TPU v7x, 32 devices: a whole 2x2x4 slice. The times are simulated.
32 devices in a mesh: pack: 8 (over z, x), seq: 4 (over y, core).
Axes of the slice: x: 2, y: 2, z: 4, core: 2. Of those that a mesh axis runs over, the one named last changes fastest.
Arguments:
- source: bfloat16 [4, 1536, 1152], P('seq', 'pack')
- destination: int32 [4, 1536], P('seq', 'pack'), may hold values from 0 to 1535, as said below
- doc_ids: int32 [8, 768], P('pack'), may hold values from 0 to 5, as said below
- w_qkv: bfloat16 [3, 1152, 1152], P(None, None, 'seq')
- w_out: bfloat16 [1152, 1152], P('seq'), may hold values from -0.1875 to 0.1875
Outputs:
- projected: bfloat16 [8, 768, 1152], P('pack', 'seq')
Inputs may be any that keep to these rules, and one draw needn't show every extreme that they name: For every column s, destination[s] is a permutation of 0 to 1535. Of the 192 rows of one device, at most 48 have the same destination // 192, and in every column some device sends exactly 48 rows to one owner. doc_ids[p] starts at 0, never falls, rises by one at most from one position to the next and changes only at positions that are multiples of 128; some packed row reaches the largest value.
All inputs are finite; a program needn't handle non-finite values.
Results may differ from a plain program's by a relative error of at most 0.011.
Values may be sent and summed in bfloat16 or wider, within the bound.
A program may use at most 64 MiB of HBM per device.

v0:
```python
import math

import jax
import jax.numpy as jnp
from jax import lax
from jax.sharding import PartitionSpec as P

HD = 72


def block_rows(length):
    best = 1
    for candidate in range(1, min(length, 512) + 1):
        if length % candidate == 0:
            best = candidate
    return best


def attend_head(queries, key_rows, value_rows, documents):
    length = queries.shape[0]
    height = block_rows(length)

    def one_block(number):
        query_blk = lax.dynamic_slice_in_dim(queries, number * height, height, 0)
        doc_blk = lax.dynamic_slice_in_dim(documents, number * height, height, 0)
        scores = jnp.einsum(
            "qc,kc->qk", query_blk, key_rows, preferred_element_type=jnp.float32
        ) / math.sqrt(HD)
        scores = jnp.where(doc_blk[:, None] == documents[None, :], scores, -jnp.inf)
        highest = jnp.max(scores, axis=1, keepdims=True)
        expo = jnp.exp(scores - highest)
        weights = (expo / jnp.sum(expo, axis=1, keepdims=True)).astype(jnp.bfloat16)
        return jnp.dot(weights, value_rows, preferred_element_type=jnp.float32).astype(jnp.bfloat16)

    blocks = lax.map(one_block, jnp.arange(length // height, dtype=jnp.int32))
    return blocks.reshape(length, queries.shape[1])


def body(source, destination, doc_ids, w_qkv, w_out):
    pack_count = lax.axis_size("pack")
    tok_dev = source.shape[1]
    width = source.shape[2]
    capacity = 2 * tok_dev // pack_count
    my_rows = source[0]
    targets = destination[0]
    owners = targets // tok_dev
    places = targets % tok_dev
    matches = owners[:, None] == jnp.arange(pack_count, dtype=jnp.int32)[None, :]
    counted = jnp.cumsum(matches.astype(jnp.int32), axis=0)
    slots = jnp.sum(jnp.where(matches, counted, 0), axis=1) - 1
    flat_slot = owners * capacity + slots
    outbox = jnp.zeros((pack_count * capacity, width), jnp.bfloat16).at[flat_slot].set(my_rows)
    labels = jnp.full((pack_count * capacity,), tok_dev, jnp.int32).at[flat_slot].set(places)
    inbox, arrived = (
        lax.all_to_all(
            outbox.reshape(pack_count, capacity, width),
            "pack",
            split_axis=0,
            concat_axis=0,
            tiled=True,
        ),
        lax.all_to_all(
            labels.reshape(pack_count, capacity), "pack", split_axis=0, concat_axis=0, tiled=True
        ),
    )
    packed = (
        jnp.zeros((tok_dev, width), jnp.bfloat16)
        .at[arrived.reshape(-1)]
        .set(inbox.reshape(-1, width), mode="drop")
    )
    local_qkv = jnp.einsum(
        "td,jdc->jtc",
        packed,
        lax.all_gather(w_qkv, "seq", axis=2, tiled=True),
        preferred_element_type=jnp.float32,
    ).astype(jnp.bfloat16)
    heads_qkv = lax.all_to_all(local_qkv, "seq", split_axis=2, concat_axis=1, tiled=True)
    documents = doc_ids[0]
    head_count = heads_qkv.shape[2] // HD
    attended_list = []
    for which in range(head_count):
        lower = which * HD
        attended_list.append(
            attend_head(
                heads_qkv[0, :, lower : lower + HD],
                heads_qkv[1, :, lower : lower + HD],
                heads_qkv[2, :, lower : lower + HD],
                documents,
            )
        )
    attended = jnp.concatenate(attended_list, axis=1)
    token_major = lax.all_to_all(attended, "seq", split_axis=0, concat_axis=1, tiled=True)
    summed = jnp.dot(
        token_major,
        lax.all_gather(w_out, "seq", axis=0, tiled=True),
        preferred_element_type=jnp.float32,
    )
    return summed.astype(jnp.bfloat16)[None]


def solution(mesh):
    placed = (
        P("seq", "pack", None),
        P("seq", "pack"),
        P("pack", None),
        P(None, None, "seq"),
        P("seq", None),
    )
    return jax.shard_map(
        body, mesh=mesh, in_specs=placed, out_specs=P("pack", "seq", None), check_vma=False
    )
```

profile of v0, /device:TPU:27, one launch (start us, length us, event | category | flops | bytes accessed | tf_op | source)
XLA Modules:
  0.0 177.1 jit_solution(1378623884114661952)
XLA Ops:
  6.5 0.7 all-gather.3.cloned.1.call-update
  8.3 1.2 scatter_custom_fusion
  9.5 0.7 all_to_all.34
  10.2 5.4 %all-to-all-start = ((s32[8,1,48]{2,1,0:T(1,128)}), s32[8,1,48]{2,1,0:T(1,128)S(1)}, u32[]{:S(2)}, u32[]{:S(2)}) async-start(s32[8,1,48]{2,1,0:T(1,128)} %all_to_all.34), calls=%async_computation | async-start | bytes 8192 | tf_op jit(solution)/shard_map/all_to_all | solution.py:62
  15.7 2.5 %scatter_custom_fusion.1 = bf16[384,1152]{1,0:T(8,128)(2,1)} fusion(s32[192]{0:T(256)S(1)} %bitcast.140, bf16[1,192,1152]{2,1,0:T(8,128)(2,1)S(1)} %copy-done, bf16[]{:T(256)} %constant.109.clone.1), kind=kCustom, calls=%fused_computation.49 | custom fusion | bytes 1327106 | tf_op jit(solution)/shard_map/scatter | solution.py:52
  18.2 6.2 %all-to-all-start.1 = ((bf16[8,48,1152]{2,1,0:T(8,128)(2,1)}), bf16[8,48,1152]{2,1,0:T(8,128)(2,1)S(1)}, u32[]{:S(2)}, u32[]{:S(2)}) async-start(bf16[8,48,1152]{2,1,0:T(8,128)(2,1)} %bitcast.18), calls=%async_computation.1 | async-start | bytes 1769472 | tf_op jit(solution)/shard_map/all_to_all | solution.py:55
  24.9 0.7 reduce.14
  25.7 19.3 %all-to-all-done.1 = bf16[8,48,1152]{2,1,0:T(8,128)(2,1)S(1)} async-done(((bf16[8,48,1152]{2,1,0:T(8,128)(2,1)}), bf16[8,48,1152]{2,1,0:T(8,128)(2,1)S(1)}, u32[]{:S(2)}, u32[]{:S(2)}) %all-to-all-start.1) | async-done | bytes 884768 | tf_op jit(solution)/shard_map/all_to_all | solution.py:55
  44.9 2.2 %scatter_custom_fusion.2 = bf16[192,1152]{1,0:T(8,128)(2,1)S(1)} fusion(s32[384]{0:T(512)S(1)} %fusion.33, bf16[384,1152]{1,0:T(8,128)(2,1)S(1)} %bitcast.135, bf16[]{:T(256)} %constant.109.clone.1), kind=kCustom, calls=%fused_computation.52 | custom fusion | bytes 442370 | tf_op jit(solution)/shard_map/scatter | solution.py:69
  47.2 19.0 %all-gather.3.cloned.1.call-done = bf16[3,1152,1152]{1,2,0:T(8,128)(2,1)} async-done(((bf16[3,1152,288]{1,2,0:T(8,128)(2,1)}), bf16[3,1152,1152]{1,2,0:T(8,128)(2,1)}) %all-gather.3.cloned.1.call-update) | async-done | bytes 7962640 | tf_op jit(solution)/shard_map/all_gather | solution.py:74
  66.2 5.7 %fusion.24 = bf16[3,192,1152]{2,1,0:T(8,128)(2,1)S(1)} fusion(bf16[3,1152,1152]{1,2,0:T(8,128)(2,1)} %all-gather.3.cloned.1.call-done, bf16[192,1152]{1,0:T(8,128)(2,1)S(1)} %scatter_custom_fusion.2), kind=kOutput, calls=%fused_computation.44 | convolution fusion | flops 1529487360 | bytes 9732096 | tf_op jit(solution)/shard_map/td,jdc->jtc/dot_general | solution.py:71
  72.0 3.2 %copy.13 = bf16[3,192,1152]{1,0,2:T(4,128)(2,1)} copy(bf16[3,192,1152]{2,1,0:T(8,128)(2,1)S(1)} %fusion.24) | data formatting | bytes 2654208 | tf_op jit(solution)/shard_map/convert_element_type | solution.py:76
  75.2 4.0 %all-to-all-start.2 = ((bf16[3,192,1152]{1,0,2:T(4,128)(2,1)}), bf16[3,192,1152]{1,0,2:T(4,128)(2,1)S(1)}, u32[]{:S(2)}, u32[]{:S(2)}) async-start(bf16[3,192,1152]{1,0,2:T(4,128)(2,1)} %copy.13), calls=%async_computation.2 | async-start | bytes 4718592 | tf_op jit(solution)/shard_map/all_to_all | solution.py:77
  79.2 0.7 all-gather.5.cloned.1.call-update
  79.9 41.0 %all-to-all-done.2 = bf16[3,192,1152]{1,0,2:T(4,128)(2,1)S(1)} async-done(((bf16[3,192,1152]{1,0,2:T(4,128)(2,1)}), bf16[3,192,1152]{1,0,2:T(4,128)(2,1)S(1)}, u32[]{:S(2)}, u32[]{:S(2)}) %all-to-all-start.2) | async-done | bytes 1327136 | tf_op jit(solution)/shard_map/all_to_all | solution.py:77
  120.9 1.4 copy-done.1
  122.4 4.2 %copy.14 = bf16[3,4,192,288]{3,2,1,0:T(8,128)(2,1)S(1)} copy(bf16[3,4,192,288]{2,0,3,1:T(4,128)(2,1)} %bitcast.133) | data formatting | bytes 2654208 | tf_op jit(solution)/shard_map/all_to_all | solution.py:77
  126.6 1.6 slice_bitcast_fusion.9
  128.2 7.2 %while.40 = (s32[]{:T(128)}, bf16[2,384,72]{1,2,0:T(8,128)(2,1)S(1)}, s32[2]{0:T(128)S(1)}, s32[768]{0:T(1024)S(1)}, s32[1,768]{1,0:T(1,128)S(1)}, /*index=5*/bf...) while((s32[]{:T(128)}, ...), condition=%wide.region_9.10_spmd, body=%wide.region_6.9_spmd.sunk | while | flops 87615744 | bytes 4550875 | solution.py:35
  128.2 0.6 dynamic_slice.66
  129.5 1.4 fusion.73
  131.8 0.6 dynamic_slice.66
  133.1 1.4 fusion.73
  135.8 5.3 %while.41 = (s32[]{:T(128)}, bf16[2,384,72]{1,2,0:T(8,128)(2,1)S(1)}, s32[2]{0:T(128)S(1)}, s32[768]{0:T(1024)S(1)}, s32[1,768]{1,0:T(1,128)S(1)}, /*index=5*/bf...) while((s32[]{:T(128)}, ...), condition=%wide.region_13.14_spmd, body=%wide.region_10.13_spmd.sunk | while | flops 87615744 | bytes 4110015 | solution.py:35
  135.8 0.6 dynamic_slice.69
  138.4 0.6 dynamic_slice.69
  141.3 5.3 %while.42 = (s32[]{:T(128)}, bf16[2,384,72]{1,2,0:T(8,128)(2,1)S(1)}, s32[2]{0:T(128)S(1)}, s32[768]{0:T(1024)S(1)}, s32[1,768]{1,0:T(1,128)S(1)}, /*index=5*/bf...) while((s32[]{:T(128)}, ...), condition=%wide.region_17.18_spmd, body=%wide.region_14.17_spmd.sunk | while | flops 87615744 | bytes 4110015 | solution.py:35
  146.9 5.3 %while.43 = (s32[]{:T(128)}, bf16[2,384,72]{1,2,0:T(8,128)(2,1)S(1)}, s32[2]{0:T(128)S(1)}, s32[768]{0:T(1024)S(1)}, s32[1,768]{1,0:T(1,128)S(1)}, /*index=5*/bf...) while((s32[]{:T(128)}, ...), condition=%wide.region_21.22_spmd, body=%wide.region_18.21_spmd.sunk | while | flops 87615744 | bytes 4110015 | solution.py:35
  153.0 0.9 copy.19
  153.9 4.4 %all-to-all-start.3 = ((bf16[4,192,288]{1,2,0:T(8,128)(2,1)}), bf16[4,192,288]{1,2,0:T(8,128)(2,1)S(1)}, u32[]{:S(2)}, u32[]{:S(2)}) async-start(bf16[4,192,288]{1,2,0:T(8,128)(2,1)} %copy.19), calls=%async_computation.3 | async-start | bytes 1179648 | tf_op jit(solution)/shard_map/all_to_all | solution.py:92
  158.3 8.7 %all-to-all-done.3 = bf16[4,192,288]{1,2,0:T(8,128)(2,1)S(1)} async-done(((bf16[4,192,288]{1,2,0:T(8,128)(2,1)}), bf16[4,192,288]{1,2,0:T(8,128)(2,1)S(1)}, u32[]{:S(2)}, u32[]{:S(2)}) %all-to-all-start.3) | async-done | bytes 442400 | tf_op jit(solution)/shard_map/all_to_all | solution.py:92
  167.0 3.3 %fusion.25 = bf16[1,192,1152]{2,1,0:T(8,128)(2,1)} fusion(bf16[192,1152]{0,1:T(8,128)(2,1)S(1)} %bitcast.134, bf16[1152,1152]{1,0:T(8,128)(2,1)} %all-gather.5.cloned.1.call-done), kind=kOutput, calls=%fused_computation.46 | convolution fusion | flops 509829120 | bytes 3538944 | tf_op jit(solution)/shard_map/dot_general | solution.py:93
  (97 shorter events, 15.8 us)
Async XLA Ops:
  6.5 9.1 %copy-start = (bf16[1,192,1152]{2,1,0:T(8,128)(2,1)S(1)}, bf16[1,192,1152]{2,1,0:T(8,128)(2,1)}, u32[]{:S(2)}) copy-start(bf16[1,192,1152]{2,1,0:T(8,128)(2,1)} %param.13) | copy-start | bytes 1327108
  6.5 0.7 copy-start.7
  6.5 59.7 %all-gather.3.cloned.1.call-start = ((), (), s32[]{:S(2)}) async-start(), calls=%async_computation.4 | async-start | bytes 9953280 | tf_op jit(solution)/shard_map/all_gather | solution.py:74
  10.2 8.0 %all-to-all-start = ((s32[8,1,48]{2,1,0:T(1,128)}), s32[8,1,48]{2,1,0:T(1,128)S(1)}, u32[]{:S(2)}, u32[]{:S(2)}) async-start(s32[8,1,48]{2,1,0:T(1,128)} %all_to_all.34), calls=%async_computation | async-start | bytes 8192 | tf_op jit(solution)/shard_map/all_to_all | solution.py:62
  18.2 26.8 %all-to-all-start.1 = ((bf16[8,48,1152]{2,1,0:T(8,128)(2,1)}), bf16[8,48,1152]{2,1,0:T(8,128)(2,1)S(1)}, u32[]{:S(2)}, u32[]{:S(2)}) async-start(bf16[8,48,1152]{2,1,0:T(8,128)(2,1)} %bitcast.18), calls=%async_computation.1 | async-start | bytes 1769472 | tf_op jit(solution)/shard_map/all_to_all | solution.py:55
  75.2 4.7 %copy-start.2 = (s32[1,768]{1,0:T(1,128)S(1)}, s32[1,768]{1,0:T(1,128)}, u32[]{:S(2)}) copy-start(s32[1,768]{1,0:T(1,128)} %param.15) | copy-start | bytes 9220
  75.2 45.8 %all-to-all-start.2 = ((bf16[3,192,1152]{1,0,2:T(4,128)(2,1)}), bf16[3,192,1152]{1,0,2:T(4,128)(2,1)S(1)}, u32[]{:S(2)}, u32[]{:S(2)}) async-start(bf16[3,192,1152]{1,0,2:T(4,128)(2,1)} %copy.13), calls=%async_computation.2 | async-start | bytes 4718592 | tf_op jit(solution)/shard_map/all_to_all | solution.py:77
  79.2 79.1 %all-gather.5.cloned.1.call-start = ((), (), s32[]{:S(2)}) async-start(), calls=%async_computation.5 | async-start | bytes 3317760 | tf_op jit(solution)/shard_map/all_gather | solution.py:95
  120.9 1.4 copy-start.1
  128.2 7.5 %copy-start.3 = (bf16[768,72]{1,0:T(8,128)(2,1)S(1)}, bf16[768,72]{1,0:T(8,128)(2,1)}, u32[]{:S(2)}) copy-start(bf16[768,72]{1,0:T(8,128)(2,1)} %get-tuple-element.556) | copy-start | bytes 331780
  128.2 7.5 %copy-start.4 = (bf16[768,72]{1,0:T(8,128)(2,1)S(1)}, bf16[768,72]{1,0:T(8,128)(2,1)}, u32[]{:S(2)}) copy-start(bf16[768,72]{1,0:T(8,128)(2,1)} %get-tuple-element.555) | copy-start | bytes 331780
  128.2 7.5 %copy-start.5 = (bf16[768,72]{1,0:T(8,128)(2,1)S(1)}, bf16[768,72]{1,0:T(8,128)(2,1)}, u32[]{:S(2)}) copy-start(bf16[768,72]{1,0:T(8,128)(2,1)} %get-tuple-element.554) | copy-start | bytes 331780
  129.5 1.8 %copy-start.6 = (bf16[768,72]{1,0:T(8,128)(2,1)S(1)}, bf16[768,72]{1,0:T(8,128)(2,1)}, u32[]{:S(2)}) copy-start(bf16[768,72]{1,0:T(8,128)(2,1)} %get-tuple-element.616) | copy-start | bytes 331780 | tf_op jit(solution)/shard_map/while
  133.1 1.8 %copy-start.6 = (bf16[768,72]{1,0:T(8,128)(2,1)S(1)}, bf16[768,72]{1,0:T(8,128)(2,1)}, u32[]{:S(2)}) copy-start(bf16[768,72]{1,0:T(8,128)(2,1)} %get-tuple-element.616) | copy-start | bytes 331780 | tf_op jit(solution)/shard_map/while
  153.9 13.1 %all-to-all-start.3 = ((bf16[4,192,288]{1,2,0:T(8,128)(2,1)}), bf16[4,192,288]{1,2,0:T(8,128)(2,1)S(1)}, u32[]{:S(2)}, u32[]{:S(2)}) async-start(bf16[4,192,288]{1,2,0:T(8,128)(2,1)} %copy.19), calls=%async_computation.3 | async-start | bytes 1179648 | tf_op jit(solution)/shard_map/all_to_all | solution.py:92
Sparse Core Ops, SparseCore 0:
  8.9 57.2 all-gather.2
  81.5 41.1 all-gather.4
where the time goes:
time: 180 us; the launch traced here: 177 us
  waiting for transfers between devices  89.4 us (50%)
  local copies, waits for them, and re-layouts  25.1 us (14%)
  starting transfers between devices  20 us (11%)
  matrix products  18.7 us (10%)
  between operations  13.7 us (8%)
  loops' own time  5.32 us (3%)
  other arithmetic  4.88 us (3%)
    all_to_all x1, waiting for transfers between devices, body(): lax.all_to_all(local_qkv, 'seq', split_axis=2, concat_axis=1, tiled=True)  41 us
    all_to_all x1, waiting for transfers between devices, body(): lax.all_to_all(outbox.reshape(pack_count, capacity, width), 'pack', split...  19.3 us
    all_gather x1, waiting for transfers between devices, body(): lax.all_gather(w_qkv, 'seq', axis=2, tiled=True)  19 us
    all_to_all x1, waiting for transfers between devices, body(): lax.all_to_all(attended, 'seq', split_axis=0, concat_axis=1, tiled=True)  8.68 us
    all_to_all x1, starting transfers between devices, body(): lax.all_to_all(outbox.reshape(pack_count, capacity, width), 'pack', split...  6.23 us
    dot_general x1, matrix products, body(): jnp.einsum('td,jdc->jtc', packed, lax.all_gather(w_qkv, 'seq', axis=2, ti...  5.74 us
    all_to_all x1, starting transfers between devices, body(): lax.all_to_all(labels.reshape(pack_count, capacity), 'pack', split_axis=0...  5.44 us
    dot_general x8, matrix products, one_block(): jnp.einsum('qc,kc->qk', query_blk, key_rows, preferred_element_type=jnp.f...  5.37 us
  transfers between devices with their start and end apart: 6, of which 4 were waited for; matrix products, arithmetic and copies ran while one was open for 19% of the time, Pallas kernels for 0%

commit v1 on v0

v1 whole, which is shorter than its diff:
```python
import functools
import math

import jax
import jax.numpy as jnp
from jax import lax
from jax.experimental import pallas as pl
from jax.experimental.pallas import tpu as pltpu
from jax.sharding import PartitionSpec as P

HD = 72
CORES = 2
MESH = pl.DeviceIdType.MESH
F32 = jnp.float32
BF16 = jnp.bfloat16


def head_window(head, group):
    lower = head * HD // 128 * 128
    upper = min(-(-(head + 1) * HD // 128) * 128, group)
    return lower, upper


def kernel(
    n, rows_y, cap, pieces,
    src, dst, doc, wqkv, wout, out,
    outbox, inbox, lab_out, lab_in, packed, acc, qkv, doc_col, att_acc, att_out, att_in, w_all,
    disp_send, disp_recv, lab_send, lab_recv,
    tok_send, tok_recv, tokf_send, tokf_recv,
    w_send, w_recv, wf_send, wf_recv, att_send, att_recv,
):
    n_seq = rows_y * CORES
    tok = src.shape[1]
    wide = src.shape[2] // pieces
    group = wout.shape[0]
    length = doc.shape[1]
    heads = group // HD
    me = lax.axis_index("pack")
    seq = lax.axis_index("seq")
    my_y, my_c = seq // CORES, seq % CORES
    sib = (me, my_y * CORES + 1 - my_c)

    def on_y(d):
        return (me, (my_y + d) % rows_y * CORES + my_c)

    def remote(source, target, ss, rs, device):
        return pltpu.make_async_remote_copy(
            src_ref=source, dst_ref=target, send_sem=ss, recv_sem=rs,
            device_id=device, device_id_type=MESH,
        )

    barrier = pltpu.get_barrier_semaphore()
    for k in range(1, n):
        pl.semaphore_signal(barrier, inc=1, device_id=((me + k) % n, seq), device_id_type=MESH)
    for k in range(1, n_seq):
        pl.semaphore_signal(barrier, inc=1, device_id=(me, (seq + k) % n_seq), device_id_type=MESH)

    dest = dst[...]
    steps = lax.broadcasted_iota(jnp.int32, (n, tok), 0)
    owners = jnp.sum((dest >= (steps + 1) * tok).astype(jnp.int32), axis=0, keepdims=True)
    places = dest - owners * tok
    shift = owners - me
    shift = jnp.where(shift < 0, shift + n, shift)
    matches = (steps == shift).astype(F32)
    before = lax.broadcasted_iota(jnp.int32, (tok, tok), 0) <= lax.broadcasted_iota(jnp.int32, (tok, tok), 1)
    counted = jnp.dot(matches.astype(BF16), before.astype(F32).astype(BF16), preferred_element_type=F32)
    slots = jnp.sum(matches * counted, axis=0, keepdims=True).astype(jnp.int32) - 1
    flat = shift * cap + slots
    chosen = (lax.broadcasted_iota(jnp.int32, (n * cap, tok), 0) == flat).astype(F32).astype(BF16)
    named = jnp.broadcast_to((places + 1).astype(F32), (8, tok)).astype(BF16)
    lab_out[...] = lax.dot_general(named, chosen, (((1,), (1,)), ((), ())), preferred_element_type=F32)

    def column(c):
        return pl.ds(c * wide, wide)

    def fill(c):
        outbox[c] = jnp.dot(chosen, src[0, :, column(c)], preferred_element_type=F32).astype(BF16)
        inbox[c, 0:cap] = outbox[c, 0:cap]

    def label_copy(k):
        return remote(lab_out, lab_in.at[k], lab_send.at[k], lab_recv.at[k], ((me + k) % n, seq))

    def dispatch_copy(c, k):
        block = pl.ds(k * cap, cap)
        return remote(
            outbox.at[c, block], inbox.at[c, block], disp_send.at[c, k], disp_recv.at[c, k],
            ((me + k) % n, seq),
        )

    def token_copy(c, d, at_y):
        place = packed.at[c, at_y, my_c]
        return remote(place, place, tok_send.at[c, d], tok_recv.at[c, d], on_y(d) if d else sib)

    def token_forward(c, d, at_c):
        place = packed.at[c, (my_y - d) % rows_y, at_c]
        return remote(place, place, tokf_send.at[c, d], tokf_recv.at[c, d], sib)

    def weight_copy(c, d):
        return remote(
            wout.at[:, column(c)], w_all.at[c, my_y, my_c], w_send.at[c, d], w_recv.at[c, d],
            on_y(d) if d else sib,
        )

    def weight_forward(c, d, at_c):
        place = w_all.at[c, (my_y - d) % rows_y, at_c]
        return remote(place, place, wf_send.at[c, d], wf_recv.at[c, d], sib)

    fill(0)
    pl.semaphore_wait(barrier, n - 1 + n_seq - 1)
    for k in range(1, n):
        label_copy(k).start()
    for c in range(pieces):
        if c:
            fill(c)
        for k in range(1, n):
            dispatch_copy(c, k).start()

    def send_weights(c):
        for d in range(1, rows_y):
            weight_copy(c, d).start()
        weight_copy(c, 0).start()

    def forward_weights(c):
        for d in range(1, rows_y):
            weight_copy(c, d).wait_recv()
            weight_forward(c, d, my_c).start()

    send_weights(0)

    doc_row = doc[...].astype(F32)
    doc_col[...] = jnp.broadcast_to(doc_row, (128, length)).T.reshape(doc_col.shape)

    lane = lax.broadcasted_iota(jnp.int32, (1, n * cap), 1)
    label = jnp.where(lane < cap, lab_out[0:1, :], 0.0)
    for k in range(1, n):
        label_copy(k).wait_recv()
        label = jnp.where((lane >= k * cap) & (lane < (k + 1) * cap), lab_in[k, 0:1, :], label)
    rows = lax.broadcasted_iota(jnp.int32, (tok, n * cap), 0) + 1
    placing = (rows.astype(F32) == label).astype(F32).astype(BF16)

    def project(c, at_y):
        block = packed[c, at_y].reshape(CORES * tok, wide)
        for j in range(3):
            part = jnp.dot(block, wqkv[j, column(c), :], preferred_element_type=F32)
            if c:
                part = part + acc[j, at_y]
            if c < pieces - 1:
                acc[j, at_y] = part
            else:
                qkv[j, at_y] = part.astype(BF16).reshape(CORES, tok, group)

    def consume(c):
        for d in range(1, rows_y):
            token_copy(c, d, (my_y - d) % rows_y).wait_recv()
            token_forward(c, d, my_c).start()
        token_copy(c, 0, my_y).wait_recv()
        project(c, my_y)
        for d in range(1, rows_y):
            token_forward(c, d, 1 - my_c).wait_recv()
            project(c, (my_y - d) % rows_y)

    for c in range(pieces):
        for k in range(1, n):
            dispatch_copy(c, k).wait_recv()
        packed[c, my_y, my_c] = jnp.dot(placing, inbox[c], preferred_element_type=F32).astype(BF16)
        for d in range(1, rows_y):
            token_copy(c, d, my_y).start()
        token_copy(c, 0, my_y).start()
        if c:
            send_weights(c)
            consume(c - 1)
            forward_weights(c - 1)
    consume(pieces - 1)

    factor = math.log2(math.e) / math.sqrt(HD)

    def target(i):
        at_y = (my_y + i // CORES + 1) % rows_y
        at_c = (my_c + 1 - i % CORES) % CORES
        return at_y, at_c

    def attended_copy(i):
        at_y, at_c = target(i)
        return remote(
            att_out.at[i], att_in.at[i], att_send.at[i], att_recv.at[i], (me, at_y * CORES + at_c)
        )

    def attend(i, carry):
        at_y, at_c = target(i)
        same = doc_col[at_y, at_c][:, 0:1] == doc_row
        att_acc[...] = jnp.zeros_like(att_acc)
        for h in range(heads):
            lower, upper = head_window(h, group)
            lanes = lax.broadcasted_iota(jnp.int32, (1, upper - lower), 1) + lower
            mine = (lanes >= h * HD) & (lanes < (h + 1) * HD)
            query = jnp.where(mine, qkv[0, at_y, at_c, :, lower:upper].astype(F32), 0.0).astype(BF16)
            keys = qkv[1, :, :, :, lower:upper].reshape(length, upper - lower)
            values = qkv[2, :, :, :, lower:upper].reshape(length, upper - lower)
            scores = lax.dot_general(query, keys, (((1,), (1,)), ((), ())), preferred_element_type=F32)
            scores = jnp.where(same, scores, -jnp.inf)
            expo = jnp.exp2((scores - jnp.max(scores, axis=1, keepdims=True)) * factor)
            total = jnp.sum(expo, axis=1, keepdims=True)
            mixed = jnp.dot(expo.astype(BF16), values, preferred_element_type=F32) / total
            att_acc[:, lower:upper] += jnp.where(mine, mixed, 0.0)
        att_out[i] = att_acc[...].astype(BF16)

        @pl.when(i < n_seq - 1)
        def _():
            attended_copy(i).start()

        return carry

    lax.fori_loop(0, n_seq, attend, 0)
    forward_weights(pieces - 1)

    own = att_out[n_seq - 1]
    totals = [jnp.dot(own, wout[:, column(c)], preferred_element_type=F32) for c in range(pieces)]
    for c in range(pieces):
        weight_copy(c, 0).wait_recv()
        for d in range(1, rows_y):
            weight_forward(c, d, 1 - my_c).wait_recv()
    for i in range(n_seq - 2, -1, -1):
        attended_copy(i).wait_recv()
        from_y = (my_y - (i // CORES + 1)) % rows_y
        from_c = (my_c - (1 - i % CORES)) % CORES
        arrived = att_in[i]
        totals = [
            totals[c] + jnp.dot(arrived, w_all[c, from_y, from_c], preferred_element_type=F32)
            for c in range(pieces)
        ]
    for c in range(pieces):
        out[0, :, column(c)] = totals[c].astype(BF16)

    for k in range(1, n):
        label_copy(k).wait_send()
    for c in range(pieces):
        for k in range(1, n):
            dispatch_copy(c, k).wait_send()
        for d in range(rows_y):
            token_copy(c, d, my_y).wait_send()
            weight_copy(c, d).wait_send()
            if d:
                token_forward(c, d, my_c).wait_send()
                weight_forward(c, d, my_c).wait_send()
    for i in range(n_seq - 1):
        attended_copy(i).wait_send()


def body(source, destination, doc_ids, w_qkv, w_out):
    n = lax.axis_size("pack")
    n_seq = lax.axis_size("seq")
    rows_y = n_seq // CORES
    tok, width = source.shape[1:]
    group = w_out.shape[0]
    length = doc_ids.shape[1]
    cap = -(-(2 * tok // n) // 16) * 16
    pieces = 3
    wide = width // pieces
    dma = pltpu.SemaphoreType.DMA
    vmem = pl.BlockSpec(memory_space=pltpu.VMEM)
    return pl.pallas_call(
        functools.partial(kernel, n, rows_y, cap, pieces),
        out_shape=jax.ShapeDtypeStruct((1, tok, width), BF16),
        in_specs=[vmem] * 5,
        out_specs=vmem,
        scratch_shapes=[
            pltpu.VMEM((pieces, n * cap, wide), BF16),
            pltpu.VMEM((pieces, n * cap, wide), BF16),
            pltpu.VMEM((8, n * cap), F32),
            pltpu.VMEM((n, 8, n * cap), F32),
            pltpu.VMEM((pieces, rows_y, CORES, tok, wide), BF16),
            pltpu.VMEM((3, rows_y, CORES * tok, group), F32),
            pltpu.VMEM((3, rows_y, CORES, tok, group), BF16),
            pltpu.VMEM((rows_y, CORES, tok, 128), F32),
            pltpu.VMEM((tok, group), F32),
            pltpu.VMEM((n_seq, tok, group), BF16),
            pltpu.VMEM((n_seq, tok, group), BF16),
            pltpu.VMEM((pieces, rows_y, CORES, group, wide), BF16),
            dma((pieces, n)), dma((pieces, n)), dma((n,)), dma((n,)),
            dma((pieces, rows_y)), dma((pieces, rows_y)), dma((pieces, rows_y)), dma((pieces, rows_y)),
            dma((pieces, rows_y)), dma((pieces, rows_y)), dma((pieces, rows_y)), dma((pieces, rows_y)),
            dma((n_seq,)), dma((n_seq,)),
        ],
        compiler_params=pltpu.CompilerParams(
            collective_id=0, has_side_effects=True, vmem_limit_bytes=56 * 1024 * 1024
        ),
        cost_estimate=pl.CostEstimate(flops=4_000_000_000, bytes_accessed=4_000_000, transcendentals=2_400_000),
    )(source, destination, doc_ids, w_qkv, w_out)


def solution(mesh):
    placed = (
        P("seq", "pack", None),
        P("seq", "pack"),
        P("pack", None),
        P(None, None, "seq"),
        P("seq", None),
    )
    return jax.shard_map(
        body, mesh=mesh, in_specs=placed, out_specs=P("pack", "seq", None), check_vma=False
    )
```

time: 180 us -> 60.4 us (0.34); the launches traced: 177 us -> 59.7 us
  waiting for transfers between devices: 89.4 us -> 0 us
  Pallas kernels: 0 us -> 53.7 us
  starting transfers between devices: 20 us -> 0 us
  local copies, waits for them, and re-layouts: 25.1 us -> 6 us
  matrix products: 18.7 us -> 0 us
  between operations: 13.7 us -> 0.01 us
  loops' own time: 5.32 us -> 0 us
  other arithmetic: 4.88 us -> 0 us
    all_to_all x4 -> x0, waiting for transfers between devices: 69 us -> none  [the longest x1 41 us: body(): lax.all_to_all(local_qkv, 'seq', split_axis=2, concat_axis=1, tiled=True)]
    pallas_call x0 -> x1, Pallas kernels: none -> 53.7 us  [body(): pl.pallas_call(functools.partial(kernel, n, rows_y, cap, pieces), out_sha...]
    all_to_all x4 -> x0, starting transfers between devices: 20 us -> none  [the longest x1 6.23 us: body(): lax.all_to_all(outbox.reshape(pack_count, capacity, width), 'pack', split...]
    all_gather x2 -> x0, waiting for transfers between devices: 19 us -> none  [the longest x1 19 us: body(): lax.all_gather(w_qkv, 'seq', axis=2, tiled=True)]
    dot_general x18 -> x0, matrix products: 18.7 us -> none  [the longest x1 5.74 us: body(): jnp.einsum('td,jdc->jtc', packed, lax.all_gather(w_qkv, 'seq', axis=2, ti...]
    scatter x3 -> x0, local copies, waits for them, and re-layouts: 5.95 us -> none  [the longest x1 2.52 us: body(): jnp.zeros((pack_count * capacity, width), jnp.bfloat16).at[flat_slot]]
    all_to_all x3 -> x0, local copies, waits for them, and re-layouts: 5.39 us -> none  [the longest x1 4.2 us: body(): lax.all_to_all(local_qkv, 'seq', split_axis=2, concat_axis=1, tiled=True)]
    dynamic_slice x16 -> x0, local copies, waits for them, and re-layouts: 5.32 us -> none  [the longest x8 4.7 us: attend_head(): blocks = lax.map(one_block, jnp.arange(length // height, dtype=jnp.int32))]
  transfers between devices with their start and end apart: 6 -> 0, of which waited for: 4 -> 0; matrix products, arithmetic and copies ran while one was open for 19% -> 0% of each run, Pallas kernels for 0% -> 0%
where the time goes in v1:
time: 60.4 us; the launch traced here: 59.7 us
  Pallas kernels  53.7 us (89%)
  local copies, waits for them, and re-layouts  6 us (10%)
    pallas_call x1, Pallas kernels, body(): pl.pallas_call(functools.partial(kernel, n, rows_y, cap, pieces), out_sha...  53.7 us
    unnamed x2, local copies, waits for them, and re-layouts  6 us

profile of v1, /device:TPU:27, one launch (start us, length us, event | category | flops | bytes accessed | tf_op | source)
XLA Modules:
  0.0 59.7 jit_solution(13796143817158633880)
XLA Ops:
  0.0 4.2 %copy.6.wqkv = bf16[3,1152,288]{2,1,0:T(8,128)(2,1)} copy(bf16[3,1152,288]{1,2,0:T(8,128)(2,1)} %param.8) | data formatting | bytes 3981312 | tf_op args[3]
  4.2 53.7 %shard_map.55 = bf16[1,192,1152]{2,1,0:T(8,128)(2,1)} custom-call(bf16[1,192,1152]{2,1,0:T(8,128)(2,1)} %src.1, s32[1,192]{1,0:T(1,128)} %dst.1, s32[1,768]{1,0:T(1,128)} %doc.1, bf16[3,1152,288]{2,1,0:T(8,128)(2,1)} %copy.6.wqkv, bf16[288,1152]{1,0:T(8,128)(2,1)} %wout.1), custom_call_target="tpu_custom_call" | custom-call | flops 4000000000 | bytes 4000000 | tf_op jit(solution)/shard_map/pallas_call | solution.py:261
  57.9 1.8 %copy.8 = bf16[1,192,1152]{2,1,0:T(8,128)(2,1)} copy(bf16[1,192,1152]{2,1,0:T(8,128)(2,1)} %shard_map.55) | data formatting | bytes 884736

commit v2 on v1

v2 whole, which is shorter than its diff:
```python
import functools
import math

import jax
import jax.numpy as jnp
from jax import lax
from jax.experimental import pallas as pl
from jax.experimental.pallas import tpu as pltpu
from jax.sharding import PartitionSpec as P

HD = 72
CORES = 2
MESH = pl.DeviceIdType.MESH
F32 = jnp.float32
BF16 = jnp.bfloat16


def head_window(head, group):
    lower = head * HD // 128 * 128
    upper = min(-(-(head + 1) * HD // 128) * 128, group)
    return lower, upper


def kernel(
    n, rows_y, cap, pieces,
    src, dst, doc, wqkv_hbm, wout_hbm, out,
    wqkv, outbox, inbox, lab_out, lab_in, packed, acc, qkv, doc_col, att_acc, att_out, att_in, w_all,
    disp_send, disp_recv, lab_send, lab_recv,
    tok_send, tok_recv, tokf_send, tokf_recv,
    w_send, w_recv, wf_send, wf_recv, att_send, att_recv, load_sem,
):
    n_seq = rows_y * CORES
    tok = src.shape[1]
    group = wout_hbm.shape[0]
    length = doc.shape[1]
    heads = group // HD
    me = lax.axis_index("pack")
    seq = lax.axis_index("seq")
    my_y, my_c = seq // CORES, seq % CORES
    sib = (me, my_y * CORES + 1 - my_c)

    def on_y(d):
        return (me, (my_y + d) % rows_y * CORES + my_c)

    def remote(source, target, ss, rs, device):
        return pltpu.make_async_remote_copy(
            src_ref=source, dst_ref=target, send_sem=ss, recv_sem=rs,
            device_id=device, device_id_type=MESH,
        )

    load_qkv = pltpu.make_async_copy(wqkv_hbm, wqkv, load_sem.at[0])
    load_out = pltpu.make_async_copy(wout_hbm, w_all.at[my_y, my_c], load_sem.at[1])
    load_out.start()
    load_qkv.start()

    barrier = pltpu.get_barrier_semaphore()
    for k in range(1, n):
        pl.semaphore_signal(barrier, inc=1, device_id=((me + k) % n, seq), device_id_type=MESH)
    for k in range(1, n_seq):
        pl.semaphore_signal(barrier, inc=1, device_id=(me, (seq + k) % n_seq), device_id_type=MESH)

    dest = dst[...]
    steps = lax.broadcasted_iota(jnp.int32, (n, tok), 0)
    owners = jnp.sum((dest >= (steps + 1) * tok).astype(jnp.int32), axis=0, keepdims=True)
    places = dest - owners * tok
    shift = owners - me
    shift = jnp.where(shift < 0, shift + n, shift)
    matches = (steps == shift).astype(F32)
    before = lax.broadcasted_iota(jnp.int32, (tok, tok), 0) <= lax.broadcasted_iota(jnp.int32, (tok, tok), 1)
    counted = jnp.dot(matches.astype(BF16), before.astype(F32).astype(BF16), preferred_element_type=F32)
    slots = jnp.sum(matches * counted, axis=0, keepdims=True).astype(jnp.int32) - 1
    flat = shift * cap + slots
    chosen = (lax.broadcasted_iota(jnp.int32, (n * cap, tok), 0) == flat).astype(F32).astype(BF16)
    named = jnp.broadcast_to((places + 1).astype(F32), (8, tok)).astype(BF16)
    lab_out[...] = lax.dot_general(named, chosen, (((1,), (1,)), ((), ())), preferred_element_type=F32)

    def column(c):
        return pl.ds(*pieces[c])

    def fill(c):
        moved = jnp.dot(chosen, src[0, :, column(c)], preferred_element_type=F32).astype(BF16)
        outbox[:, column(c)] = moved
        inbox[0:cap, column(c)] = moved[0:cap]

    def label_copy(k):
        return remote(lab_out, lab_in.at[k], lab_send.at[k], lab_recv.at[k], ((me + k) % n, seq))

    def dispatch_copy(c, k):
        block = pl.ds(k * cap, cap)
        return remote(
            outbox.at[block, column(c)], inbox.at[block, column(c)], disp_send.at[c, k], disp_recv.at[c, k],
            ((me + k) % n, seq),
        )

    def token_copy(c, d, at_y):
        place = packed.at[at_y, my_c, :, column(c)]
        return remote(place, place, tok_send.at[c, d], tok_recv.at[c, d], on_y(d) if d else sib)

    def token_forward(c, d, at_c):
        place = packed.at[(my_y - d) % rows_y, at_c, :, column(c)]
        return remote(place, place, tokf_send.at[c, d], tokf_recv.at[c, d], sib)

    def weight_copy(c, d):
        place = w_all.at[my_y, my_c, :, column(c)]
        return remote(place, place, w_send.at[c, d], w_recv.at[c, d], on_y(d) if d else sib)

    def weight_forward(c, d, at_c):
        place = w_all.at[(my_y - d) % rows_y, at_c, :, column(c)]
        return remote(place, place, wf_send.at[c, d], wf_recv.at[c, d], sib)

    fill(0)
    pl.semaphore_wait(barrier, n - 1 + n_seq - 1)
    for k in range(1, n):
        label_copy(k).start()
    for c in range(len(pieces)):
        if c:
            fill(c)
        for k in range(1, n):
            dispatch_copy(c, k).start()

    def send_weights(c):
        for d in range(1, rows_y):
            weight_copy(c, d).start()
        weight_copy(c, 0).start()

    def forward_weights(c):
        for d in range(1, rows_y):
            weight_copy(c, d).wait_recv()
            weight_forward(c, d, my_c).start()

    load_out.wait()
    send_weights(0)

    doc_row = doc[...].astype(F32)
    doc_col[...] = jnp.broadcast_to(doc_row, (128, length)).T.reshape(doc_col.shape)

    lane = lax.broadcasted_iota(jnp.int32, (1, n * cap), 1)
    label = jnp.where(lane < cap, lab_out[0:1, :], 0.0)
    for k in range(1, n):
        label_copy(k).wait_recv()
        label = jnp.where((lane >= k * cap) & (lane < (k + 1) * cap), lab_in[k, 0:1, :], label)
    rows = lax.broadcasted_iota(jnp.int32, (tok, n * cap), 0) + 1
    placing = (rows.astype(F32) == label).astype(F32).astype(BF16)

    def project(c, at_y):
        block = packed[at_y, :, :, column(c)].reshape(CORES * tok, pieces[c][1])
        for j in range(3):
            part = lax.dot_general(
                block, wqkv[j, :, column(c)], (((1,), (1,)), ((), ())), preferred_element_type=F32
            )
            if c:
                part = part + acc[j, at_y]
            if c < len(pieces) - 1:
                acc[j, at_y] = part
            else:
                qkv[j, at_y] = part.astype(BF16).reshape(CORES, tok, group)

    def consume(c):
        for d in range(1, rows_y):
            token_copy(c, d, (my_y - d) % rows_y).wait_recv()
            token_forward(c, d, my_c).start()
        token_copy(c, 0, my_y).wait_recv()
        project(c, my_y)
        for d in range(1, rows_y):
            token_forward(c, d, 1 - my_c).wait_recv()
            project(c, (my_y - d) % rows_y)

    load_qkv.wait()
    for c in range(len(pieces)):
        for k in range(1, n):
            dispatch_copy(c, k).wait_recv()
        packed[my_y, my_c, :, column(c)] = jnp.dot(
            placing, inbox[:, column(c)], preferred_element_type=F32
        ).astype(BF16)
        for d in range(1, rows_y):
            token_copy(c, d, my_y).start()
        token_copy(c, 0, my_y).start()
        if c:
            send_weights(c)
            consume(c - 1)
            forward_weights(c - 1)
    consume(len(pieces) - 1)

    factor = math.log2(math.e) / math.sqrt(HD)

    def attended_copy(i, at_c, to):
        return remote(
            att_out.at[i, at_c], att_in.at[i, my_c], att_send.at[i, at_c], att_recv.at[i, my_c], to
        )

    def arrival(i, at_c):
        place = att_in.at[i, at_c]
        return remote(place, place, att_send.at[i, at_c], att_recv.at[i, at_c], sib)

    def attend(i, carry):
        at_y = (my_y + i + 1) % rows_y
        same = doc_col[at_y][:, 0:1] == doc_row
        att_acc[...] = jnp.zeros_like(att_acc)
        for h in range(heads):
            lower, upper = head_window(h, group)
            lanes = lax.broadcasted_iota(jnp.int32, (1, upper - lower), 1) + lower
            mine = (lanes >= h * HD) & (lanes < (h + 1) * HD)
            query = qkv[0, at_y, :, :, lower:upper].reshape(CORES * tok, upper - lower)
            query = jnp.where(mine, query.astype(F32), 0.0).astype(BF16)
            keys = qkv[1, :, :, :, lower:upper].reshape(length, upper - lower)
            values = qkv[2, :, :, :, lower:upper].reshape(length, upper - lower)
            scores = lax.dot_general(query, keys, (((1,), (1,)), ((), ())), preferred_element_type=F32)
            scores = jnp.where(same, scores, -jnp.inf)
            expo = jnp.exp2((scores - jnp.max(scores, axis=1, keepdims=True)) * factor)
            total = jnp.sum(expo, axis=1, keepdims=True)
            mixed = jnp.dot(expo.astype(BF16), values, preferred_element_type=F32) / total
            att_acc[:, lower:upper] += jnp.where(mine, mixed, 0.0)
        att_out[i] = att_acc[...].astype(BF16).reshape(CORES, tok, group)

        @pl.when(i < rows_y - 1)
        def _():
            for at_c in range(CORES):
                attended_copy(i, at_c, (me, at_y * CORES + at_c)).start()

        return carry

    lax.fori_loop(0, rows_y, attend, 0)
    last = rows_y - 1
    attended_copy(last, 1 - my_c, sib).start()
    forward_weights(len(pieces) - 1)

    def mixed_out(rows, at_y, at_c):
        return jnp.dot(rows, w_all[at_y, at_c], preferred_element_type=F32)

    total = mixed_out(att_out[last, my_c], my_y, my_c)
    for c in range(len(pieces)):
        weight_copy(c, 0).wait_recv()
        for d in range(1, rows_y):
            weight_forward(c, d, 1 - my_c).wait_recv()
    for i in range(rows_y - 1):
        for at_c in range(CORES):
            arrival(i, at_c).wait_recv()
            total = total + mixed_out(att_in[i, at_c], (my_y - i - 1) % rows_y, at_c)
    arrival(last, 1 - my_c).wait_recv()
    total = total + mixed_out(att_in[last, 1 - my_c], my_y, 1 - my_c)
    out[0] = total.astype(BF16)

    for k in range(1, n):
        label_copy(k).wait_send()
    for c in range(len(pieces)):
        for k in range(1, n):
            dispatch_copy(c, k).wait_send()
        for d in range(rows_y):
            token_copy(c, d, my_y).wait_send()
            weight_copy(c, d).wait_send()
            if d:
                token_forward(c, d, my_c).wait_send()
                weight_forward(c, d, my_c).wait_send()
    for i in range(rows_y - 1):
        for at_c in range(CORES):
            attended_copy(i, at_c, sib).wait_send()
    attended_copy(last, 1 - my_c, sib).wait_send()


def body(source, destination, doc_ids, w_qkv, w_out):
    n = lax.axis_size("pack")
    n_seq = lax.axis_size("seq")
    rows_y = n_seq // CORES
    tok, width = source.shape[1:]
    group = w_out.shape[0]
    length = doc_ids.shape[1]
    cap = -(-(2 * tok // n) // 16) * 16
    tiles = width // 128
    ends = [0, tiles - tiles * 5 // 9, tiles - tiles * 2 // 9, tiles]
    pieces = [(start * 128, (end - start) * 128) for start, end in zip(ends, ends[1:])]
    parts = len(pieces)
    dma = pltpu.SemaphoreType.DMA
    vmem = pl.BlockSpec(memory_space=pltpu.VMEM)
    return pl.pallas_call(
        functools.partial(kernel, n, rows_y, cap, pieces),
        out_shape=jax.ShapeDtypeStruct((1, tok, width), BF16),
        in_specs=[vmem] * 3 + [pl.BlockSpec(memory_space=pl.ANY)] * 2,
        out_specs=vmem,
        scratch_shapes=[
            pltpu.VMEM((3, group, width), BF16),
            pltpu.VMEM((n * cap, width), BF16),
            pltpu.VMEM((n * cap, width), BF16),
            pltpu.VMEM((8, n * cap), F32),
            pltpu.VMEM((n, 8, n * cap), F32),
            pltpu.VMEM((rows_y, CORES, tok, width), BF16),
            pltpu.VMEM((3, rows_y, CORES * tok, group), F32),
            pltpu.VMEM((3, rows_y, CORES, tok, group), BF16),
            pltpu.VMEM((rows_y, CORES * tok, 128), F32),
            pltpu.VMEM((CORES * tok, group), F32),
            pltpu.VMEM((rows_y, CORES, tok, group), BF16),
            pltpu.VMEM((rows_y, CORES, tok, group), BF16),
            pltpu.VMEM((rows_y, CORES, group, width), BF16),
            dma((parts, n)), dma((parts, n)), dma((n,)), dma((n,)),
            dma((parts, rows_y)), dma((parts, rows_y)), dma((parts, rows_y)), dma((parts, rows_y)),
            dma((parts, rows_y)), dma((parts, rows_y)), dma((parts, rows_y)), dma((parts, rows_y)),
            dma((rows_y, CORES)), dma((rows_y, CORES)), dma((2,)),
        ],
        compiler_params=pltpu.CompilerParams(
            collective_id=0, has_side_effects=True, vmem_limit_bytes=56 * 1024 * 1024
        ),
        cost_estimate=pl.CostEstimate(flops=4_000_000_000, bytes_accessed=4_000_000, transcendentals=2_400_000),
    )(source, destination, doc_ids, jnp.swapaxes(w_qkv, 1, 2), w_out)


def solution(mesh):
    placed = (
        P("seq", "pack", None),
        P("seq", "pack"),
        P("pack", None),
        P(None, None, "seq"),
        P("seq", None),
    )
    return jax.shard_map(
        body, mesh=mesh, in_specs=placed, out_specs=P("pack", "seq", None), check_vma=False
    )
```

time: 60.4 us -> 56 us (0.927)
  local copies, waits for them, and re-layouts: 6 us -> 1.81 us
    unnamed x2 -> x1, local copies, waits for them, and re-layouts: 6 us -> 1.81 us
where the time goes in v2:
time: 56 us; the launch traced here: 55.1 us
  Pallas kernels  53.3 us (95%)
  local copies, waits for them, and re-layouts  1.81 us (3%)
    pallas_call x1, Pallas kernels, body(): pl.pallas_call(functools.partial(kernel, n, rows_y, cap, pieces), out_sha...  53.3 us
    unnamed x1, local copies, waits for them, and re-layouts  1.81 us

profile of v2, /device:TPU:27, one launch (start us, length us, event | category | flops | bytes accessed | tf_op | source)
XLA Modules:
  0.0 55.1 jit_solution(7312707492504240188)
XLA Ops:
  0.0 53.3 %shard_map.55 = bf16[1,192,1152]{2,1,0:T(8,128)(2,1)} custom-call(bf16[1,192,1152]{2,1,0:T(8,128)(2,1)} %src.1, s32[1,192]{1,0:T(1,128)} %dst.1, s32[1,768]{1,0:T(1,128)} %doc.1, bf16[3,288,1152]{2,1,0:T(8,128)(2,1)} %bitcast.1, bf16[288,1152]{1,0:T(8,128)(2,1)} %wout_hbm.1), custom_call_target="tpu_custom_call" | custom-call | flops 4000000000 | bytes 4000000 | tf_op jit(solution)/shard_map/pallas_call | solution.py:274
  53.3 1.8 %copy.7 = bf16[1,192,1152]{2,1,0:T(8,128)(2,1)} copy(bf16[1,192,1152]{2,1,0:T(8,128)(2,1)} %shard_map.55) | data formatting | bytes 884736

commit v3 on v2

--- a/solution.py
+++ b/solution.py
@@ -112,11 +112,8 @@
     pl.semaphore_wait(barrier, n - 1 + n_seq - 1)
     for k in range(1, n):
         label_copy(k).start()
-    for c in range(len(pieces)):
-        if c:
-            fill(c)
-        for k in range(1, n):
-            dispatch_copy(c, k).start()
+    for k in range(1, n):
+        dispatch_copy(0, k).start()
 
     def send_weights(c):
         for d in range(1, rows_y):
@@ -129,7 +126,10 @@
             weight_forward(c, d, my_c).start()
 
     load_out.wait()
-    send_weights(0)
+    for c in range(len(pieces)):
+        send_weights(c)
+    for c in range(1, len(pieces)):
+        fill(c)
 
     doc_row = doc[...].astype(F32)
     doc_col[...] = jnp.broadcast_to(doc_row, (128, length)).T.reshape(doc_col.shape)
@@ -168,6 +168,10 @@
     load_qkv.wait()
     for c in range(len(pieces)):
         for k in range(1, n):
+            dispatch_copy(c, k).wait_send()
+            if c + 1 < len(pieces):
+                dispatch_copy(c + 1, k).start()
+        for k in range(1, n):
             dispatch_copy(c, k).wait_recv()
         packed[my_y, my_c, :, column(c)] = jnp.dot(
             placing, inbox[:, column(c)], preferred_element_type=F32
@@ -176,7 +180,6 @@
             token_copy(c, d, my_y).start()
         token_copy(c, 0, my_y).start()
         if c:
-            send_weights(c)
             consume(c - 1)
             forward_weights(c - 1)
     consume(len(pieces) - 1)
@@ -243,8 +246,6 @@
     for k in range(1, n):
         label_copy(k).wait_send()
     for c in range(len(pieces)):
-        for k in range(1, n):
-            dispatch_copy(c, k).wait_send()
         for d in range(rows_y):
             token_copy(c, d, my_y).wait_send()
             weight_copy(c, d).wait_send()

time: 56 us -> 53.2 us (0.950); the launches traced: 55.1 us -> 53 us
  Pallas kernels: 53.3 us -> 51.2 us
    pallas_call x1, Pallas kernels: 53.3 us -> 51.2 us  [body(): pl.pallas_call(functools.partial(kernel, n, rows_y, cap, pieces), out_sha...]
where the time goes in v3:
time: 53.2 us; the launch traced here: 53 us
  Pallas kernels  51.2 us (96%)
  local copies, waits for them, and re-layouts  1.81 us (3%)
    pallas_call x1, Pallas kernels, body(): pl.pallas_call(functools.partial(kernel, n, rows_y, cap, pieces), out_sha...  51.2 us
    unnamed x1, local copies, waits for them, and re-layouts  1.81 us

profile of v3, /device:TPU:27, one launch (start us, length us, event | category | flops | bytes accessed | tf_op | source)
XLA Modules:
  0.0 53.0 jit_solution(14837498567011792184)
XLA Ops:
  0.0 51.2 %shard_map.55 = bf16[1,192,1152]{2,1,0:T(8,128)(2,1)} custom-call(bf16[1,192,1152]{2,1,0:T(8,128)(2,1)} %src.1, s32[1,192]{1,0:T(1,128)} %dst.1, s32[1,768]{1,0:T(1,128)} %doc.1, bf16[3,288,1152]{2,1,0:T(8,128)(2,1)} %bitcast.1, bf16[288,1152]{1,0:T(8,128)(2,1)} %wout_hbm.1), custom_call_target="tpu_custom_call" | custom-call | flops 4000000000 | bytes 4000000 | tf_op jit(solution)/shard_map/pallas_call | solution.py:275
  51.2 1.8 %copy.7 = bf16[1,192,1152]{2,1,0:T(8,128)(2,1)} copy(bf16[1,192,1152]{2,1,0:T(8,128)(2,1)} %shard_map.55) | data formatting | bytes 884736

commit v4 on v2

--- a/solution.py
+++ b/solution.py
@@ -24,7 +24,7 @@
 def kernel(
     n, rows_y, cap, pieces,
     src, dst, doc, wqkv_hbm, wout_hbm, out,
-    wqkv, outbox, inbox, lab_out, lab_in, packed, acc, qkv, doc_col, att_acc, att_out, att_in, w_all,
+    wqkv, outbox, inbox, lab_out, lab_in, packed, acc, qkv, doc_col, bias, att_acc, att_out, att_in, w_all,
     disp_send, disp_recv, lab_send, lab_recv,
     tok_send, tok_recv, tokf_send, tokf_recv,
     w_send, w_recv, wf_send, wf_recv, att_send, att_recv, load_sem,
@@ -129,7 +129,8 @@
             weight_forward(c, d, my_c).start()
 
     load_out.wait()
-    send_weights(0)
+    for c in range(len(pieces)):
+        send_weights(c)
 
     doc_row = doc[...].astype(F32)
     doc_col[...] = jnp.broadcast_to(doc_row, (128, length)).T.reshape(doc_col.shape)
@@ -141,6 +142,8 @@
         label = jnp.where((lane >= k * cap) & (lane < (k + 1) * cap), lab_in[k, 0:1, :], label)
     rows = lax.broadcasted_iota(jnp.int32, (tok, n * cap), 0) + 1
     placing = (rows.astype(F32) == label).astype(F32).astype(BF16)
+
+    factor = math.log2(math.e) / math.sqrt(HD)
 
     def project(c, at_y):
         block = packed[at_y, :, :, column(c)].reshape(CORES * tok, pieces[c][1])
@@ -153,6 +156,8 @@
             if c < len(pieces) - 1:
                 acc[j, at_y] = part
             else:
+                if j == 0:
+                    part = part * factor
                 qkv[j, at_y] = part.astype(BF16).reshape(CORES, tok, group)
 
     def consume(c):
@@ -176,12 +181,9 @@
             token_copy(c, d, my_y).start()
         token_copy(c, 0, my_y).start()
         if c:
-            send_weights(c)
             consume(c - 1)
             forward_weights(c - 1)
     consume(len(pieces) - 1)
-
-    factor = math.log2(math.e) / math.sqrt(HD)
 
     def attended_copy(i, at_c, to):
         return remote(
@@ -194,7 +196,7 @@
 
     def attend(i, carry):
         at_y = (my_y + i + 1) % rows_y
-        same = doc_col[at_y][:, 0:1] == doc_row
+        bias[...] = jnp.where(doc_col[at_y][:, 0:1] == doc_row, 0.0, -jnp.inf)
         att_acc[...] = jnp.zeros_like(att_acc)
         for h in range(heads):
             lower, upper = head_window(h, group)
@@ -205,10 +207,10 @@
             keys = qkv[1, :, :, :, lower:upper].reshape(length, upper - lower)
             values = qkv[2, :, :, :, lower:upper].reshape(length, upper - lower)
             scores = lax.dot_general(query, keys, (((1,), (1,)), ((), ())), preferred_element_type=F32)
-            scores = jnp.where(same, scores, -jnp.inf)
-            expo = jnp.exp2((scores - jnp.max(scores, axis=1, keepdims=True)) * factor)
-            total = jnp.sum(expo, axis=1, keepdims=True)
-            mixed = jnp.dot(expo.astype(BF16), values, preferred_element_type=F32) / total
+            scores = scores + bias[...]
+            expo = jnp.exp2(scores - jnp.max(scores, axis=1, keepdims=True))
+            share = 1.0 / jnp.sum(expo, axis=1, keepdims=True)
+            mixed = jnp.dot(expo.astype(BF16), values, preferred_element_type=F32) * share
             att_acc[:, lower:upper] += jnp.where(mine, mixed, 0.0)
         att_out[i] = att_acc[...].astype(BF16).reshape(CORES, tok, group)
 
@@ -255,6 +257,10 @@
         for at_c in range(CORES):
             attended_copy(i, at_c, sib).wait_send()
     attended_copy(last, 1 - my_c, sib).wait_send()
+
+
+def pass_on(given, out):
+    out[...] = given[...]
 
 
 def body(source, destination, doc_ids, w_qkv, w_out):
@@ -271,7 +277,7 @@
     parts = len(pieces)
     dma = pltpu.SemaphoreType.DMA
     vmem = pl.BlockSpec(memory_space=pltpu.VMEM)
-    return pl.pallas_call(
+    result = pl.pallas_call(
         functools.partial(kernel, n, rows_y, cap, pieces),
         out_shape=jax.ShapeDtypeStruct((1, tok, width), BF16),
         in_specs=[vmem] * 3 + [pl.BlockSpec(memory_space=pl.ANY)] * 2,
@@ -286,6 +292,7 @@
             pltpu.VMEM((3, rows_y, CORES * tok, group), F32),
             pltpu.VMEM((3, rows_y, CORES, tok, group), BF16),
             pltpu.VMEM((rows_y, CORES * tok, 128), F32),
+            pltpu.VMEM((CORES * tok, length), F32),
             pltpu.VMEM((CORES * tok, group), F32),
             pltpu.VMEM((rows_y, CORES, tok, group), BF16),
             pltpu.VMEM((rows_y, CORES, tok, group), BF16),
@@ -300,6 +307,9 @@
         ),
         cost_estimate=pl.CostEstimate(flops=4_000_000_000, bytes_accessed=4_000_000, transcendentals=2_400_000),
     )(source, destination, doc_ids, jnp.swapaxes(w_qkv, 1, 2), w_out)
+    return pl.pallas_call(
+        pass_on, out_shape=jax.ShapeDtypeStruct(result.shape, BF16), in_specs=[vmem], out_specs=vmem
+    )(result)
 
 
 def solution(mesh):

time: 56 us -> 53.2 us (0.950); the launches traced: 55.1 us -> 53 us
  local copies, waits for them, and re-layouts: 1.81 us -> 0 us
    pallas_call x1, Pallas kernels: 53.3 us -> 51.2 us  [body(): pl.pallas_call(functools.partial(kernel, n, rows_y, cap, pieces), out_sha...]
    unnamed x1 -> x0, local copies, waits for them, and re-layouts: 1.81 us -> none
    pallas_call x0 -> x1, Pallas kernels: none -> 1.81 us  [body(): pl.pallas_call(pass_on, out_shape=jax.ShapeDtypeStruct(result.shape, BF16...]
where the time goes in v4:
time: 53.2 us; the launch traced here: 53 us
  Pallas kernels  53 us (100%)
    pallas_call x1, Pallas kernels, body(): pl.pallas_call(functools.partial(kernel, n, rows_y, cap, pieces), out_sha...  51.2 us
    pallas_call x1, Pallas kernels, body(): pl.pallas_call(pass_on, out_shape=jax.ShapeDtypeStruct(result.shape, BF16...  1.81 us

profile of v4, /device:TPU:27, one launch (start us, length us, event | category | flops | bytes accessed | tf_op | source)
XLA Modules:
  0.0 53.0 jit_solution(6434361693472612852)
XLA Ops:
  0.0 51.2 %shard_map.55.given = bf16[1,192,1152]{2,1,0:T(8,128)(2,1)} custom-call(bf16[1,192,1152]{2,1,0:T(8,128)(2,1)} %src.1, s32[1,192]{1,0:T(1,128)} %dst.1, s32[1,768]{1,0:T(1,128)} %doc.1, bf16[3,288,1152]{2,1,0:T(8,128)(2,1)} %bitcast.1, bf16[288,1152]{1,0:T(8,128)(2,1)} %wout_hbm.1), custom_call_target="tpu_custom_call" | custom-call | flops 4000000000 | bytes 4000000 | tf_op jit(solution)/shard_map/pallas_call | solution.py:280
  51.2 1.8 %shard_map.56 = bf16[1,192,1152]{2,1,0:T(8,128)(2,1)} custom-call(bf16[1,192,1152]{2,1,0:T(8,128)(2,1)} %shard_map.55.given), custom_call_target="tpu_custom_call" | custom-call | tf_op jit(solution)/shard_map/pallas_call | solution.py:310

commit v5 on v4

--- a/solution.py
+++ b/solution.py
@@ -24,7 +24,7 @@
 def kernel(
     n, rows_y, cap, pieces,
     src, dst, doc, wqkv_hbm, wout_hbm, out,
-    wqkv, outbox, inbox, lab_out, lab_in, packed, acc, qkv, doc_col, bias, att_acc, att_out, att_in, w_all,
+    wqkv, outbox, inbox, lab_out, lab_in, packed, acc, qkv, doc_col, bias, att_acc, att_out, att_in, rest_out, rest_in, w_all,
     disp_send, disp_recv, lab_send, lab_recv,
     tok_send, tok_recv, tokf_send, tokf_recv,
     w_send, w_recv, wf_send, wf_recv, att_send, att_recv, load_sem,
@@ -129,7 +129,7 @@
             weight_forward(c, d, my_c).start()
 
     load_out.wait()
-    for c in range(len(pieces)):
+    for c in range(len(pieces) - 1):
         send_weights(c)
 
     doc_row = doc[...].astype(F32)
@@ -183,16 +183,27 @@
         if c:
             consume(c - 1)
             forward_weights(c - 1)
+    send_weights(len(pieces) - 1)
     consume(len(pieces) - 1)
 
-    def attended_copy(i, at_c, to):
-        return remote(
-            att_out.at[i, at_c], att_in.at[i, my_c], att_send.at[i, at_c], att_recv.at[i, my_c], to
-        )
-
-    def arrival(i, at_c):
-        place = att_in.at[i, at_c]
-        return remote(place, place, att_send.at[i, at_c], att_recv.at[i, at_c], sib)
+    tiles = group // 128
+    rest = group - tiles * 128
+    fold = tok // rest_out.shape[2]
+
+    def tile(t):
+        return pl.ds(t * 128, 128)
+
+    def attended_copy(i, at_c, t, to):
+        if t < tiles:
+            source, place = att_out.at[i, at_c, :, tile(t)], att_in.at[i, my_c, :, tile(t)]
+        else:
+            source, place = rest_out.at[i, at_c], rest_in.at[i, my_c]
+        return remote(source, place, att_send.at[i, at_c, t], att_recv.at[i, my_c, t], to)
+
+    def arrived(i, at_c):
+        for t in range(tiles + 1):
+            place = att_in.at[i, at_c, :, tile(t)] if t < tiles else rest_in.at[i, at_c]
+            remote(place, place, att_send.at[i, at_c, t], att_recv.at[i, at_c, t], sib).wait_recv()
 
     def attend(i, carry):
         at_y = (my_y + i + 1) % rows_y
@@ -212,34 +223,52 @@
             share = 1.0 / jnp.sum(expo, axis=1, keepdims=True)
             mixed = jnp.dot(expo.astype(BF16), values, preferred_element_type=F32) * share
             att_acc[:, lower:upper] += jnp.where(mine, mixed, 0.0)
-        att_out[i] = att_acc[...].astype(BF16).reshape(CORES, tok, group)
-
-        @pl.when(i < rows_y - 1)
-        def _():
-            for at_c in range(CORES):
-                attended_copy(i, at_c, (me, at_y * CORES + at_c)).start()
+            ready = [t for t in range(tiles) if h * HD < (t + 1) * 128 <= (h + 1) * HD]
+            for t in ready:
+                att_out[i, :, :, tile(t)] = att_acc[:, tile(t)].astype(BF16).reshape(CORES, tok, 128)
+            if h == heads - 1:
+                spare = att_acc[:, tiles * 128 : group].reshape(CORES, fold, tok // fold, rest)
+                spare = jnp.concatenate([spare[:, j] for j in range(fold)], axis=2)
+                rest_out[i] = spare.astype(BF16)
+                ready = ready + [tiles]
+
+            @pl.when(i < rows_y - 1)
+            def _():
+                for t in ready:
+                    for at_c in range(CORES):
+                        attended_copy(i, at_c, t, (me, at_y * CORES + at_c)).start()
 
         return carry
 
     lax.fori_loop(0, rows_y, attend, 0)
     last = rows_y - 1
-    attended_copy(last, 1 - my_c, sib).start()
+    for t in range(tiles + 1):
+        attended_copy(last, 1 - my_c, t, sib).start()
     forward_weights(len(pieces) - 1)
 
-    def mixed_out(rows, at_y, at_c):
-        return jnp.dot(rows, w_all[at_y, at_c], preferred_element_type=F32)
-
-    total = mixed_out(att_out[last, my_c], my_y, my_c)
+    def mixed_out(rows, spare, at_y, at_c):
+        spare = spare.astype(F32)
+        spare = jnp.concatenate([spare[:, j * rest : (j + 1) * rest] for j in range(fold)], axis=0)
+        product = jnp.dot(
+            spare.astype(BF16), w_all[at_y, at_c, tiles * 128 : group, :], preferred_element_type=F32
+        )
+        if tiles:
+            product = product + jnp.dot(
+                rows[:, : tiles * 128], w_all[at_y, at_c, : tiles * 128, :], preferred_element_type=F32
+            )
+        return product
+
+    total = mixed_out(att_out[last, my_c], rest_out[last, my_c], my_y, my_c)
     for c in range(len(pieces)):
         weight_copy(c, 0).wait_recv()
         for d in range(1, rows_y):
             weight_forward(c, d, 1 - my_c).wait_recv()
     for i in range(rows_y - 1):
         for at_c in range(CORES):
-            arrival(i, at_c).wait_recv()
-            total = total + mixed_out(att_in[i, at_c], (my_y - i - 1) % rows_y, at_c)
-    arrival(last, 1 - my_c).wait_recv()
-    total = total + mixed_out(att_in[last, 1 - my_c], my_y, 1 - my_c)
+            arrived(i, at_c)
+            total = total + mixed_out(att_in[i, at_c], rest_in[i, at_c], (my_y - i - 1) % rows_y, at_c)
+    arrived(last, 1 - my_c)
+    total = total + mixed_out(att_in[last, 1 - my_c], rest_in[last, 1 - my_c], my_y, 1 - my_c)
     out[0] = total.astype(BF16)
 
     for k in range(1, n):
@@ -255,8 +284,10 @@
                 weight_forward(c, d, my_c).wait_send()
     for i in range(rows_y - 1):
         for at_c in range(CORES):
-            attended_copy(i, at_c, sib).wait_send()
-    attended_copy(last, 1 - my_c, sib).wait_send()
+            for t in range(tiles + 1):
+                attended_copy(i, at_c, t, sib).wait_send()
+    for t in range(tiles + 1):
+        attended_copy(last, 1 - my_c, t, sib).wait_send()
 
 
 def pass_on(given, out):
@@ -275,6 +306,8 @@
     ends = [0, tiles - tiles * 5 // 9, tiles - tiles * 2 // 9, tiles]
     pieces = [(start * 128, (end - start) * 128) for start, end in zip(ends, ends[1:])]
     parts = len(pieces)
+    rest = group % 128
+    fold = 128 // rest
     dma = pltpu.SemaphoreType.DMA
     vmem = pl.BlockSpec(memory_space=pltpu.VMEM)
     result = pl.pallas_call(
@@ -296,11 +329,13 @@
             pltpu.VMEM((CORES * tok, group), F32),
             pltpu.VMEM((rows_y, CORES, tok, group), BF16),
             pltpu.VMEM((rows_y, CORES, tok, group), BF16),
+            pltpu.VMEM((rows_y, CORES, tok // fold, rest * fold), BF16),
+            pltpu.VMEM((rows_y, CORES, tok // fold, rest * fold), BF16),
             pltpu.VMEM((rows_y, CORES, group, width), BF16),
             dma((parts, n)), dma((parts, n)), dma((n,)), dma((n,)),
             dma((parts, rows_y)), dma((parts, rows_y)), dma((parts, rows_y)), dma((parts, rows_y)),
             dma((parts, rows_y)), dma((parts, rows_y)), dma((parts, rows_y)), dma((parts, rows_y)),
-            dma((rows_y, CORES)), dma((rows_y, CORES)), dma((2,)),
+            dma((rows_y, CORES, group // 128 + 1)), dma((rows_y, CORES, group // 128 + 1)), dma((2,)),
         ],
         compiler_params=pltpu.CompilerParams(
             collective_id=0, has_side_effects=True, vmem_limit_bytes=56 * 1024 * 1024

time: 53.2 us -> 50.8 us (0.955)
  Pallas kernels: 53 us -> 50.6 us
    pallas_call x1, Pallas kernels: 51.2 us -> 48.8 us  [body(): pl.pallas_call(functools.partial(kernel, n, rows_y, cap, pieces), out_sha...]
where the time goes in v5:
time: 50.8 us; the launch traced here: 50.6 us
  Pallas kernels  50.6 us (100%)
    pallas_call x1, Pallas kernels, body(): pl.pallas_call(functools.partial(kernel, n, rows_y, cap, pieces), out_sha...  48.8 us
    pallas_call x1, Pallas kernels, body(): pl.pallas_call(pass_on, out_shape=jax.ShapeDtypeStruct(result.shape, BF16...  1.81 us

profile of v5, /device:TPU:27, one launch (start us, length us, event | category | flops | bytes accessed | tf_op | source)
XLA Modules:
  0.0 50.6 jit_solution(1108921500252052745)
XLA Ops:
  0.0 48.8 %shard_map.55.given = bf16[1,192,1152]{2,1,0:T(8,128)(2,1)} custom-call(bf16[1,192,1152]{2,1,0:T(8,128)(2,1)} %src.1, s32[1,192]{1,0:T(1,128)} %dst.1, s32[1,768]{1,0:T(1,128)} %doc.1, bf16[3,288,1152]{2,1,0:T(8,128)(2,1)} %bitcast.1, bf16[288,1152]{1,0:T(8,128)(2,1)} %wout_hbm.1), custom_call_target="tpu_custom_call" | custom-call | flops 4000000000 | bytes 4000000 | tf_op jit(solution)/shard_map/pallas_call | solution.py:313
  48.8 1.8 %shard_map.56 = bf16[1,192,1152]{2,1,0:T(8,128)(2,1)} custom-call(bf16[1,192,1152]{2,1,0:T(8,128)(2,1)} %shard_map.55.given), custom_call_target="tpu_custom_call" | custom-call | tf_op jit(solution)/shard_map/pallas_call | solution.py:345

commit v6 on v5

--- a/solution.py
+++ b/solution.py
@@ -10,6 +10,7 @@
 
 HD = 72
 CORES = 2
+AHEAD = 2
 MESH = pl.DeviceIdType.MESH
 F32 = jnp.float32
 BF16 = jnp.bfloat16
@@ -30,6 +31,7 @@
     w_send, w_recv, wf_send, wf_recv, att_send, att_recv, load_sem,
 ):
     n_seq = rows_y * CORES
+    early = len(pieces) * 3 // 5
     tok = src.shape[1]
     group = wout_hbm.shape[0]
     length = doc.shape[1]
@@ -112,7 +114,7 @@
     pl.semaphore_wait(barrier, n - 1 + n_seq - 1)
     for k in range(1, n):
         label_copy(k).start()
-    for c in range(len(pieces)):
+    for c in range(AHEAD):
         if c:
             fill(c)
         for k in range(1, n):
@@ -129,8 +131,10 @@
             weight_forward(c, d, my_c).start()
 
     load_out.wait()
-    for c in range(len(pieces) - 1):
+    for c in range(early):
         send_weights(c)
+    for c in range(AHEAD, len(pieces)):
+        fill(c)
 
     doc_row = doc[...].astype(F32)
     doc_col[...] = jnp.broadcast_to(doc_row, (128, length)).T.reshape(doc_col.shape)
@@ -173,6 +177,10 @@
     load_qkv.wait()
     for c in range(len(pieces)):
         for k in range(1, n):
+            dispatch_copy(c, k).wait_send()
+            if c + AHEAD < len(pieces):
+                dispatch_copy(c + AHEAD, k).start()
+        for k in range(1, n):
             dispatch_copy(c, k).wait_recv()
         packed[my_y, my_c, :, column(c)] = jnp.dot(
             placing, inbox[:, column(c)], preferred_element_type=F32
@@ -182,8 +190,10 @@
         token_copy(c, 0, my_y).start()
         if c:
             consume(c - 1)
-            forward_weights(c - 1)
-    send_weights(len(pieces) - 1)
+            if c - 1 < early:
+                forward_weights(c - 1)
+    for c in range(early, len(pieces)):
+        send_weights(c)
     consume(len(pieces) - 1)
 
     tiles = group // 128
@@ -244,7 +254,8 @@
     last = rows_y - 1
     for t in range(tiles + 1):
         attended_copy(last, 1 - my_c, t, sib).start()
-    forward_weights(len(pieces) - 1)
+    for c in range(early, len(pieces)):
+        forward_weights(c)
 
     def mixed_out(rows, spare, at_y, at_c):
         spare = spare.astype(F32)
@@ -274,8 +285,6 @@
     for k in range(1, n):
         label_copy(k).wait_send()
     for c in range(len(pieces)):
-        for k in range(1, n):
-            dispatch_copy(c, k).wait_send()
         for d in range(rows_y):
             token_copy(c, d, my_y).wait_send()
             weight_copy(c, d).wait_send()
@@ -302,9 +311,7 @@
     group = w_out.shape[0]
     length = doc_ids.shape[1]
     cap = -(-(2 * tok // n) // 16) * 16
-    tiles = width // 128
-    ends = [0, tiles - tiles * 5 // 9, tiles - tiles * 2 // 9, tiles]
-    pieces = [(start * 128, (end - start) * 128) for start, end in zip(ends, ends[1:])]
+    pieces = [(start, min(256, width - start)) for start in range(0, width, 256)]
     parts = len(pieces)
     rest = group % 128
     fold = 128 // rest

time: 50.8 us -> 50.4 us (level)
  no operation moved by 1% of the time
where the time goes in v6:
time: 50.4 us; the launch traced here: 50.2 us
  Pallas kernels  50.2 us (100%)
    pallas_call x1, Pallas kernels, body(): pl.pallas_call(functools.partial(kernel, n, rows_y, cap, pieces), out_sha...  48.4 us
    pallas_call x1, Pallas kernels, body(): pl.pallas_call(pass_on, out_shape=jax.ShapeDtypeStruct(result.shape, BF16...  1.81 us

profile of v6, /device:TPU:27, one launch (start us, length us, event | category | flops | bytes accessed | tf_op | source)
XLA Modules:
  0.0 50.2 jit_solution(9309550705732670653)
XLA Ops:
  0.0 48.4 %shard_map.55.given = bf16[1,192,1152]{2,1,0:T(8,128)(2,1)} custom-call(bf16[1,192,1152]{2,1,0:T(8,128)(2,1)} %src.1, s32[1,192]{1,0:T(1,128)} %dst.1, s32[1,768]{1,0:T(1,128)} %doc.1, bf16[3,288,1152]{2,1,0:T(8,128)(2,1)} %bitcast.1, bf16[288,1152]{1,0:T(8,128)(2,1)} %wout_hbm.1), custom_call_target="tpu_custom_call" | custom-call | flops 4000000000 | bytes 4000000 | tf_op jit(solution)/shard_map/pallas_call | solution.py:320
  48.4 1.8 %shard_map.56 = bf16[1,192,1152]{2,1,0:T(8,128)(2,1)} custom-call(bf16[1,192,1152]{2,1,0:T(8,128)(2,1)} %shard_map.55.given), custom_call_target="tpu_custom_call" | custom-call | tf_op jit(solution)/shard_map/pallas_call | solution.py:352

commit v7 on v5

--- a/solution.py
+++ b/solution.py
@@ -23,8 +23,8 @@
 
 def kernel(
     n, rows_y, cap, pieces,
-    src, dst, doc, wqkv_hbm, wout_hbm, out,
-    wqkv, outbox, inbox, lab_out, lab_in, packed, acc, qkv, doc_col, bias, att_acc, att_out, att_in, rest_out, rest_in, w_all,
+    src_hbm, dst_hbm, doc_hbm, wqkv_hbm, wout_hbm, out,
+    src, dst, doc, wqkv, outbox, inbox, lab_out, lab_in, packed, acc, qkv, doc_col, bias, att_acc, att_out, att_in, rest_out, rest_in, w_all,
     disp_send, disp_recv, lab_send, lab_recv,
     tok_send, tok_recv, tokf_send, tokf_recv,
     w_send, w_recv, wf_send, wf_recv, att_send, att_recv, load_sem,
@@ -39,6 +39,12 @@
     my_y, my_c = seq // CORES, seq % CORES
     sib = (me, my_y * CORES + 1 - my_c)
 
+    half = n // 2
+    turns = [*range(half, n), *range(1, half)]
+
+    def peer(k):
+        return ((me // half + k // half) % 2 * half + (me % half + k % half) % half, seq)
+
     def on_y(d):
         return (me, (my_y + d) % rows_y * CORES + my_c)
 
@@ -50,21 +56,31 @@
 
     load_qkv = pltpu.make_async_copy(wqkv_hbm, wqkv, load_sem.at[0])
     load_out = pltpu.make_async_copy(wout_hbm, w_all.at[my_y, my_c], load_sem.at[1])
+    loads = [
+        pltpu.make_async_copy(given, held, load_sem.at[j + 2])
+        for j, (given, held) in enumerate([(dst_hbm, dst), (src_hbm, src), (doc_hbm, doc)])
+    ]
+    for load in loads:
+        load.start()
     load_out.start()
     load_qkv.start()
 
     barrier = pltpu.get_barrier_semaphore()
     for k in range(1, n):
-        pl.semaphore_signal(barrier, inc=1, device_id=((me + k) % n, seq), device_id_type=MESH)
+        pl.semaphore_signal(barrier, inc=1, device_id=peer(k), device_id_type=MESH)
     for k in range(1, n_seq):
         pl.semaphore_signal(barrier, inc=1, device_id=(me, (seq + k) % n_seq), device_id_type=MESH)
 
+    for load in loads:
+        load.wait()
     dest = dst[...]
     steps = lax.broadcasted_iota(jnp.int32, (n, tok), 0)
     owners = jnp.sum((dest >= (steps + 1) * tok).astype(jnp.int32), axis=0, keepdims=True)
     places = dest - owners * tok
-    shift = owners - me
-    shift = jnp.where(shift < 0, shift + n, shift)
+    other = (owners >= half).astype(jnp.int32)
+    shift = owners - other * half - me % half
+    shift = jnp.where(shift < 0, shift + half, shift)
+    shift = shift + jnp.where(other == me // half, 0, half)
     matches = (steps == shift).astype(F32)
     before = lax.broadcasted_iota(jnp.int32, (tok, tok), 0) <= lax.broadcasted_iota(jnp.int32, (tok, tok), 1)
     counted = jnp.dot(matches.astype(BF16), before.astype(F32).astype(BF16), preferred_element_type=F32)
@@ -83,13 +99,13 @@
         inbox[0:cap, column(c)] = moved[0:cap]
 
     def label_copy(k):
-        return remote(lab_out, lab_in.at[k], lab_send.at[k], lab_recv.at[k], ((me + k) % n, seq))
+        return remote(lab_out, lab_in.at[k], lab_send.at[k], lab_recv.at[k], peer(k))
 
     def dispatch_copy(c, k):
         block = pl.ds(k * cap, cap)
         return remote(
             outbox.at[block, column(c)], inbox.at[block, column(c)], disp_send.at[c, k], disp_recv.at[c, k],
-            ((me + k) % n, seq),
+            peer(k),
         )
 
     def token_copy(c, d, at_y):
@@ -107,6 +123,16 @@
     def weight_forward(c, d, at_c):
         place = w_all.at[(my_y - d) % rows_y, at_c, :, column(c)]
         return remote(place, place, wf_send.at[c, d], wf_recv.at[c, d], sib)
+
+    def send_weights(c):
+        for d in range(1, rows_y):
+            weight_copy(c, d).start()
+        weight_copy(c, 0).start()
+
+    def forward_weights(c):
+        for d in range(1, rows_y):
+            weight_copy(c, d).wait_recv()
+            weight_forward(c, d, my_c).start()
 
     fill(0)
     pl.semaphore_wait(barrier, n - 1 + n_seq - 1)
@@ -115,22 +141,12 @@
     for c in range(len(pieces)):
         if c:
             fill(c)
-        for k in range(1, n):
+        for k in turns:
             dispatch_copy(c, k).start()
-
-    def send_weights(c):
-        for d in range(1, rows_y):
-            weight_copy(c, d).start()
-        weight_copy(c, 0).start()
-
-    def forward_weights(c):
-        for d in range(1, rows_y):
-            weight_copy(c, d).wait_recv()
-            weight_forward(c, d, my_c).start()
-
-    load_out.wait()
-    for c in range(len(pieces) - 1):
-        send_weights(c)
+        if c == 0:
+            load_out.wait()
+        if c < len(pieces) - 1:
+            send_weights(c)
 
     doc_row = doc[...].astype(F32)
     doc_col[...] = jnp.broadcast_to(doc_row, (128, length)).T.reshape(doc_col.shape)
@@ -313,9 +329,12 @@
     result = pl.pallas_call(
         functools.partial(kernel, n, rows_y, cap, pieces),
         out_shape=jax.ShapeDtypeStruct((1, tok, width), BF16),
-        in_specs=[vmem] * 3 + [pl.BlockSpec(memory_space=pl.ANY)] * 2,
+        in_specs=[pl.BlockSpec(memory_space=pl.ANY)] * 5,
         out_specs=vmem,
         scratch_shapes=[
+            pltpu.VMEM(source.shape, BF16),
+            pltpu.VMEM(destination.shape, jnp.int32),
+            pltpu.VMEM(doc_ids.shape, jnp.int32),
             pltpu.VMEM((3, group, width), BF16),
             pltpu.VMEM((n * cap, width), BF16),
             pltpu.VMEM((n * cap, width), BF16),
@@ -335,7 +354,7 @@
             dma((parts, n)), dma((parts, n)), dma((n,)), dma((n,)),
             dma((parts, rows_y)), dma((parts, rows_y)), dma((parts, rows_y)), dma((parts, rows_y)),
             dma((parts, rows_y)), dma((parts, rows_y)), dma((parts, rows_y)), dma((parts, rows_y)),
-            dma((rows_y, CORES, group // 128 + 1)), dma((rows_y, CORES, group // 128 + 1)), dma((2,)),
+            dma((rows_y, CORES, group // 128 + 1)), dma((rows_y, CORES, group // 128 + 1)), dma((5,)),
         ],
         compiler_params=pltpu.CompilerParams(
             collective_id=0, has_side_effects=True, vmem_limit_bytes=56 * 1024 * 1024

time: 50.8 us -> 52.2 us (1.028)
  the two profiles are of different devices: /device:TPU:27 before, /device:TPU:0 now
where the time goes in v7:
time: 52.2 us; the launch traced here: 52 us
  Pallas kernels  52 us (100%)
    pallas_call x1, Pallas kernels, body(): pl.pallas_call(functools.partial(kernel, n, rows_y, cap, pieces), out_sha...  50.2 us
    pallas_call x1, Pallas kernels, body(): pl.pallas_call(pass_on, out_shape=jax.ShapeDtypeStruct(result.shape, BF16...  1.81 us

profile of v7, /device:TPU:0, one launch (start us, length us, event | category | flops | bytes accessed | tf_op | source)
XLA Modules:
  0.0 52.0 jit_solution(9220825788755428638)
XLA Ops:
  0.0 50.2 %shard_map.55.given = bf16[1,192,1152]{2,1,0:T(8,128)(2,1)} custom-call(bf16[1,192,1152]{2,1,0:T(8,128)(2,1)} %src_hbm.1, s32[1,192]{1,0:T(1,128)} %dst_hbm.1, s32[1,768]{1,0:T(1,128)} %doc_hbm.1, bf16[3,288,1152]{2,1,0:T(8,128)(2,1)} %bitcast.1, bf16[288,1152]{1,0:T(8,128)(2,1)} %wout_hbm.1), custom_call_target="tpu_custom_call" | custom-call | flops 4000000000 | bytes 4000000 | tf_op jit(solution)/shard_map/pallas_call | solution.py:329
  50.2 1.8 %shard_map.56 = bf16[1,192,1152]{2,1,0:T(8,128)(2,1)} custom-call(bf16[1,192,1152]{2,1,0:T(8,128)(2,1)} %shard_map.55.given), custom_call_target="tpu_custom_call" | custom-call | tf_op jit(solution)/shard_map/pallas_call | solution.py:364

commit v8 on v7

--- a/solution.py
+++ b/solution.py
@@ -10,6 +10,7 @@
 
 HD = 72
 CORES = 2
+AHEAD = 2
 MESH = pl.DeviceIdType.MESH
 F32 = jnp.float32
 BF16 = jnp.bfloat16
@@ -141,8 +142,9 @@
     for c in range(len(pieces)):
         if c:
             fill(c)
-        for k in turns:
-            dispatch_copy(c, k).start()
+        if c < AHEAD:
+            for k in turns:
+                dispatch_copy(c, k).start()
         if c == 0:
             load_out.wait()
         if c < len(pieces) - 1:
@@ -188,6 +190,10 @@
 
     load_qkv.wait()
     for c in range(len(pieces)):
+        for k in turns:
+            dispatch_copy(c, k).wait_send()
+            if c + AHEAD < len(pieces):
+                dispatch_copy(c + AHEAD, k).start()
         for k in range(1, n):
             dispatch_copy(c, k).wait_recv()
         packed[my_y, my_c, :, column(c)] = jnp.dot(
@@ -290,8 +296,6 @@
     for k in range(1, n):
         label_copy(k).wait_send()
     for c in range(len(pieces)):
-        for k in range(1, n):
-            dispatch_copy(c, k).wait_send()
         for d in range(rows_y):
             token_copy(c, d, my_y).wait_send()
             weight_copy(c, d).wait_send()

time: 52.2 us -> 52.2 us (level)
  no operation moved by 1% of the time
where the time goes in v8:
time: 52.2 us; the launch traced here: 52 us
  Pallas kernels  52 us (100%)
    pallas_call x1, Pallas kernels, body(): pl.pallas_call(functools.partial(kernel, n, rows_y, cap, pieces), out_sha...  50.2 us
    pallas_call x1, Pallas kernels, body(): pl.pallas_call(pass_on, out_shape=jax.ShapeDtypeStruct(result.shape, BF16...  1.81 us

profile of v8, /device:TPU:0, one launch (start us, length us, event | category | flops | bytes accessed | tf_op | source)
XLA Modules:
  0.0 52.0 jit_solution(8394176108990615699)
XLA Ops:
  0.0 50.2 %shard_map.55.given = bf16[1,192,1152]{2,1,0:T(8,128)(2,1)} custom-call(bf16[1,192,1152]{2,1,0:T(8,128)(2,1)} %src_hbm.1, s32[1,192]{1,0:T(1,128)} %dst_hbm.1, s32[1,768]{1,0:T(1,128)} %doc_hbm.1, bf16[3,288,1152]{2,1,0:T(8,128)(2,1)} %bitcast.1, bf16[288,1152]{1,0:T(8,128)(2,1)} %wout_hbm.1), custom_call_target="tpu_custom_call" | custom-call | flops 4000000000 | bytes 4000000 | tf_op jit(solution)/shard_map/pallas_call | solution.py:333
  50.2 1.8 %shard_map.56 = bf16[1,192,1152]{2,1,0:T(8,128)(2,1)} custom-call(bf16[1,192,1152]{2,1,0:T(8,128)(2,1)} %shard_map.55.given), custom_call_target="tpu_custom_call" | custom-call | tf_op jit(solution)/shard_map/pallas_call | solution.py:368

commit v9 on v8

--- a/solution.py
+++ b/solution.py
@@ -31,6 +31,7 @@
     w_send, w_recv, wf_send, wf_recv, att_send, att_recv, load_sem,
 ):
     n_seq = rows_y * CORES
+    early = len(pieces) * 3 // 5
     tok = src.shape[1]
     group = wout_hbm.shape[0]
     length = doc.shape[1]
@@ -147,7 +148,7 @@
                 dispatch_copy(c, k).start()
         if c == 0:
             load_out.wait()
-        if c < len(pieces) - 1:
+        if c < early:
             send_weights(c)
 
     doc_row = doc[...].astype(F32)
@@ -204,8 +205,10 @@
         token_copy(c, 0, my_y).start()
         if c:
             consume(c - 1)
-            forward_weights(c - 1)
-    send_weights(len(pieces) - 1)
+            if c - 1 < early:
+                forward_weights(c - 1)
+    for c in range(early, len(pieces)):
+        send_weights(c)
     consume(len(pieces) - 1)
 
     tiles = group // 128
@@ -266,7 +269,8 @@
     last = rows_y - 1
     for t in range(tiles + 1):
         attended_copy(last, 1 - my_c, t, sib).start()
-    forward_weights(len(pieces) - 1)
+    for c in range(early, len(pieces)):
+        forward_weights(c)
 
     def mixed_out(rows, spare, at_y, at_c):
         spare = spare.astype(F32)
@@ -322,9 +326,7 @@
     group = w_out.shape[0]
     length = doc_ids.shape[1]
     cap = -(-(2 * tok // n) // 16) * 16
-    tiles = width // 128
-    ends = [0, tiles - tiles * 5 // 9, tiles - tiles * 2 // 9, tiles]
-    pieces = [(start * 128, (end - start) * 128) for start, end in zip(ends, ends[1:])]
+    pieces = [(start, min(256, width - start)) for start in range(0, width, 256)]
     parts = len(pieces)
     rest = group % 128
     fold = 128 // rest

time: 52.2 us -> 51.7 us (level)
  no operation moved by 1% of the time
where the time goes in v9:
time: 51.7 us; the launch traced here: 51.6 us
  Pallas kernels  51.6 us (100%)
    pallas_call x1, Pallas kernels, body(): pl.pallas_call(functools.partial(kernel, n, rows_y, cap, pieces), out_sha...  49.8 us
    pallas_call x1, Pallas kernels, body(): pl.pallas_call(pass_on, out_shape=jax.ShapeDtypeStruct(result.shape, BF16...  1.81 us

profile of v9, /device:TPU:0, one launch (start us, length us, event | category | flops | bytes accessed | tf_op | source)
XLA Modules:
  0.0 51.6 jit_solution(7232325036347708435)
XLA Ops:
  0.0 49.8 %shard_map.55.given = bf16[1,192,1152]{2,1,0:T(8,128)(2,1)} custom-call(bf16[1,192,1152]{2,1,0:T(8,128)(2,1)} %src_hbm.1, s32[1,192]{1,0:T(1,128)} %dst_hbm.1, s32[1,768]{1,0:T(1,128)} %doc_hbm.1, bf16[3,288,1152]{2,1,0:T(8,128)(2,1)} %bitcast.1, bf16[288,1152]{1,0:T(8,128)(2,1)} %wout_hbm.1), custom_call_target="tpu_custom_call" | custom-call | flops 4000000000 | bytes 4000000 | tf_op jit(solution)/shard_map/pallas_call | solution.py:335
  49.8 1.8 %shard_map.56 = bf16[1,192,1152]{2,1,0:T(8,128)(2,1)} custom-call(bf16[1,192,1152]{2,1,0:T(8,128)(2,1)} %shard_map.55.given), custom_call_target="tpu_custom_call" | custom-call | tf_op jit(solution)/shard_map/pallas_call | solution.py:370
